TPU v7x, 32 devices: a whole 2x2x4 slice. The times are simulated.
32 devices in a mesh: fsdp: 32 (over z, y, x, core).
Axes of the slice: x: 2, y: 2, z: 4, core: 2. Of those that a mesh axis runs over, the one named last changes fastest.
Arguments:
- tokens: bfloat16 [4096, 768], P('fsdp'), may hold values from -6 to 6
- lengths: int32 [64, 2], P('fsdp'), may hold values from 0 to 64, as said below
- cotangent: bfloat16 [4096, 768], P('fsdp'), may hold values from -6 to 6
- qkv_weight: bfloat16 [1769472], P('fsdp'), may hold values from -0.21875 to 0.21875
- out_weight: bfloat16 [589824], P('fsdp'), may hold values from -0.625 to 0.625
- up_weight: bfloat16 [2359296], P('fsdp'), may hold values from -0.21875 to 0.21875
- down_weight: bfloat16 [2359296], P('fsdp'), may hold values from -0.15625 to 0.15625
- norm_gains: bfloat16 [1536], P('fsdp'), may hold values from 0.5 to 1.5
- biases: bfloat16 [7680], P('fsdp'), may hold values from -1.796875 to 1.796875
Outputs:
- block_out: bfloat16 [4096, 768], P('fsdp')
- grad_tokens: bfloat16 [4096, 768], P('fsdp')
- grad_qkv: float32 [1769472], P('fsdp')
- grad_out_weight: float32 [589824], P('fsdp')
- grad_up: float32 [2359296], P('fsdp')
- grad_down: float32 [2359296], P('fsdp')
- grad_gains: float32 [1536], P('fsdp')
- grad_biases: float32 [7680], P('fsdp')
Inputs may be any that keep to these rules, and one draw needn't show every extreme that they name: `lengths`: in each micro-batch of 64 rows the first sequence has 1 or more tokens and the two together fill 64 // 2 to 64 rows; the rows after them are padding. In every draw some micro-batch holds one sequence of 64 tokens.
All inputs are finite; a program needn't handle non-finite values.
Results may differ from a plain program's by a relative error of at most 0.01.
Values may be sent and summed in bfloat16 or wider, within the bound.
A program may use at most 192 MiB of HBM per device.

v0:
```python
import jax
import jax.numpy as jnp
from jax import lax
from jax.sharding import PartitionSpec as P

D = 768
H = 12
HD = 64
FF = 3072
ROWS = 64
MB = 2


EPSILON = 1e-05
NEGATIVE = -1e30


def layer_norm(values, gain_vec, shift_vec):
    center = values - jnp.mean(values, axis=-1, keepdims=True)
    spread = jnp.mean(center * center, axis=-1, keepdims=True)
    return center * lax.rsqrt(spread + EPSILON) * gain_vec + shift_vec


def gelu_tanh(values):
    return (
        0.5
        * values
        * (1.0 + jnp.tanh(0.7978845608028654 * (values + 0.044715 * values * values * values)))
    )


def fetch_params(qkv_part, out_part, up_part, down_part, gain_part, bias_part):
    return (
        lax.all_gather(qkv_part, "fsdp", axis=0, tiled=True),
        lax.all_gather(out_part, "fsdp", axis=0, tiled=True),
        lax.all_gather(up_part, "fsdp", axis=0, tiled=True),
        lax.all_gather(down_part, "fsdp", axis=0, tiled=True),
        lax.all_gather(gain_part, "fsdp", axis=0, tiled=True),
        lax.all_gather(bias_part, "fsdp", axis=0, tiled=True),
    )


def unpack(gathered):
    qkv_flat, out_flat, up_flat, down_flat, gain_flat, bias_flat = gathered
    shift_all = bias_flat.astype(jnp.float32)
    return (
        qkv_flat.reshape(D, 3 * D),
        out_flat.reshape(D, D),
        up_flat.reshape(D, FF),
        down_flat.reshape(FF, D),
        gain_flat.astype(jnp.float32).reshape(2, D),
        shift_all[: 6 * D].reshape(6, D),
        shift_all[6 * D :],
    )


def micro_mask(length_pair):
    position = jnp.arange(ROWS, dtype=jnp.int32)
    first_len = length_pair[0]
    live_end = length_pair[0] + length_pair[1]
    segment = (position >= first_len).astype(jnp.int32) + (position >= live_end).astype(jnp.int32)
    allowed = (position[None, :] <= position[:, None]) & (segment[None, :] == segment[:, None])
    live_rows = (position < live_end).astype(jnp.float32)[:, None]
    return (allowed, live_rows)


def col_sum(values):
    return jnp.sum(values.astype(jnp.float32), axis=0)


def weight_grads(saved):
    (
        normed,
        grad_mixed,
        context,
        grad_attn_low,
        normed_two,
        grad_pre_low,
        activated,
        grad_out_low,
        gain_terms,
        shift_terms,
    ) = saved
    grad_qkv_w = jnp.einsum("rd,re->de", normed, grad_mixed, preferred_element_type=jnp.float32)
    grad_out_w = jnp.einsum("rd,re->de", context, grad_attn_low, preferred_element_type=jnp.float32)
    grad_up_w = jnp.einsum(
        "rd,rf->df", normed_two, grad_pre_low, preferred_element_type=jnp.float32
    )
    grad_down_w = jnp.einsum(
        "rf,rd->fd", activated, grad_out_low, preferred_element_type=jnp.float32
    )
    grad_gain = gain_terms.reshape(-1)
    grad_shift = jnp.concatenate(
        [
            shift_terms.reshape(-1),
            col_sum(grad_mixed[:, :D]),
            col_sum(grad_mixed[:, 2 * D :]),
            col_sum(grad_attn_low),
            col_sum(grad_out_low),
            col_sum(grad_pre_low),
        ]
    )
    return (grad_qkv_w, grad_out_w, grad_up_w, grad_down_w, grad_gain, grad_shift)


def pack(local, owners):
    small = jnp.concatenate([local[4].reshape(owners, -1), local[5].reshape(owners, -1)], axis=1)
    return (
        local[0].reshape(owners, -1),
        local[1].reshape(owners, -1),
        local[2].reshape(owners, -1),
        local[3].reshape(owners, -1),
        small,
    )


def unpack_grads(pieces, owners):
    gain_width = 2 * D // owners
    small = pieces[4].reshape(-1)
    return (
        pieces[0].reshape(-1),
        pieces[1].reshape(-1),
        pieces[2].reshape(-1),
        pieces[3].reshape(-1),
        small[:gain_width],
        small[gain_width:],
    )


def shards(
    tokens, lengths, cotangent, qkv_weight, out_weight, up_weight, down_weight, norm_gains, biases
):
    score_scale = HD ** (-0.5)
    owners = lax.axis_size("fsdp")
    shard_sums = None
    out_blocks = []
    grad_blocks = []
    saved_all = []
    for slot_index in range(MB):
        forward_set = fetch_params(
            qkv_weight, out_weight, up_weight, down_weight, norm_gains, biases
        )
        w_qkv, w_out, w_up, w_down, gain_rows, shift_rows, up_bias = unpack(forward_set)
        allowed, live_rows = micro_mask(lengths[slot_index])
        token_rows = tokens[slot_index * ROWS : (slot_index + 1) * ROWS].astype(jnp.float32)
        normed_f, norm_one_back = jax.vjp(layer_norm, token_rows, gain_rows[0], shift_rows[0])
        normed = normed_f.astype(jnp.bfloat16)
        qkv_mixed = jnp.dot(normed, w_qkv, preferred_element_type=jnp.float32)
        queries = (qkv_mixed[:, :D] + shift_rows[2]).astype(jnp.bfloat16).reshape(ROWS, H, HD)
        key_rows = qkv_mixed[:, D : 2 * D].astype(jnp.bfloat16).reshape(ROWS, H, HD)
        values = (qkv_mixed[:, 2 * D :] + shift_rows[3]).astype(jnp.bfloat16).reshape(ROWS, H, HD)
        scores = (
            jnp.einsum("qhe,khe->hqk", queries, key_rows, preferred_element_type=jnp.float32)
            * score_scale
        )
        scores = jnp.where(allowed[None], scores, NEGATIVE)
        row_peak = jnp.max(scores, axis=-1, keepdims=True)
        unnormed = jnp.exp(scores - row_peak)
        row_total = jnp.sum(unnormed, axis=-1, keepdims=True)
        probs_low = (unnormed / row_total).astype(jnp.bfloat16)
        logsum = row_peak + jnp.log(row_total)
        context = jnp.einsum("hqk,khe->qhe", probs_low, values, preferred_element_type=jnp.float32)
        context = context.reshape(ROWS, D).astype(jnp.bfloat16)
        residual = (
            token_rows + jnp.dot(context, w_out, preferred_element_type=jnp.float32) + shift_rows[4]
        )
        normed_two_f, norm_two_back = jax.vjp(layer_norm, residual, gain_rows[1], shift_rows[1])
        normed_two = normed_two_f.astype(jnp.bfloat16)
        pre_act = jnp.dot(normed_two, w_up, preferred_element_type=jnp.float32) + up_bias
        activated_f, gelu_back = jax.vjp(gelu_tanh, pre_act)
        activated = activated_f.astype(jnp.bfloat16)
        block_rows = (
            residual
            + jnp.dot(activated, w_down, preferred_element_type=jnp.float32)
            + shift_rows[5]
        )
        out_blocks.append((live_rows * block_rows).astype(jnp.bfloat16))
        backward_set = fetch_params(
            qkv_weight, out_weight, up_weight, down_weight, norm_gains, biases
        )
        w_qkv, w_out, w_up, w_down, gain_rows, shift_rows, up_bias = unpack(backward_set)
        grad_out = live_rows * cotangent[slot_index * ROWS : (slot_index + 1) * ROWS].astype(
            jnp.float32
        )
        grad_out_low = grad_out.astype(jnp.bfloat16)
        grad_act = jnp.einsum("rd,fd->rf", grad_out_low, w_down, preferred_element_type=jnp.float32)
        (grad_pre,) = gelu_back(grad_act)
        grad_pre_low = grad_pre.astype(jnp.bfloat16)
        grad_normed_two = jnp.einsum(
            "rf,df->rd", grad_pre_low, w_up, preferred_element_type=jnp.float32
        )
        grad_resid_norm, grad_gain_two, grad_shift_two = norm_two_back(grad_normed_two)
        grad_resid = grad_out + grad_resid_norm
        grad_attn_low = grad_resid.astype(jnp.bfloat16)
        grad_context = jnp.einsum(
            "re,de->rd", grad_attn_low, w_out, preferred_element_type=jnp.float32
        )
        grad_context = grad_context.astype(jnp.bfloat16).reshape(ROWS, H, HD)
        again = (
            jnp.einsum("qhe,khe->hqk", queries, key_rows, preferred_element_type=jnp.float32)
            * score_scale
        )
        probabilities = jnp.where(allowed[None], jnp.exp(again - logsum), 0.0)
        grad_probs = jnp.einsum(
            "qhe,khe->hqk", grad_context, values, preferred_element_type=jnp.float32
        )
        grad_values = jnp.einsum(
            "hqk,qhe->khe",
            probabilities.astype(jnp.bfloat16),
            grad_context,
            preferred_element_type=jnp.float32,
        )
        grad_values = grad_values.astype(jnp.bfloat16)
        row_delta = jnp.sum(grad_probs * probabilities, axis=-1, keepdims=True)
        grad_scores = (probabilities * (grad_probs - row_delta)).astype(jnp.bfloat16)
        grad_queries = (
            jnp.einsum("hqk,khe->qhe", grad_scores, key_rows, preferred_element_type=jnp.float32)
            * score_scale
        ).astype(jnp.bfloat16)
        grad_keys = (
            jnp.einsum("hqk,qhe->khe", grad_scores, queries, preferred_element_type=jnp.float32)
            * score_scale
        ).astype(jnp.bfloat16)
        grad_mixed = jnp.concatenate(
            [
                grad_queries.reshape(ROWS, D),
                grad_keys.reshape(ROWS, D),
                grad_values.reshape(ROWS, D),
            ],
            axis=1,
        )
        grad_normed = jnp.einsum("re,de->rd", grad_mixed, w_qkv, preferred_element_type=jnp.float32)
        grad_rows_norm, grad_gain_one, grad_shift_one = norm_one_back(grad_normed)
        grad_blocks.append((grad_resid + grad_rows_norm).astype(jnp.bfloat16))
        saved = (
            normed,
            grad_mixed,
            context,
            grad_attn_low,
            normed_two,
            grad_pre_low,
            activated,
            grad_out_low,
            jnp.stack([grad_gain_one, grad_gain_two]),
            jnp.stack([grad_shift_one, grad_shift_two]),
        )
        saved_all.append(saved)
    joined = tuple(
        (
            (
                jnp.concatenate([item[pos] for item in saved_all], axis=0)
                if pos < 8
                else sum((item[pos] for item in saved_all[1:])) + saved_all[0][pos]
            )
            for pos in range(10)
        )
    )
    packed = pack(weight_grads(joined), owners)
    shard_sums = (
        lax.psum_scatter(packed[0], "fsdp", scatter_dimension=0, tiled=True),
        lax.psum_scatter(packed[1], "fsdp", scatter_dimension=0, tiled=True),
        lax.psum_scatter(packed[2], "fsdp", scatter_dimension=0, tiled=True),
        lax.psum_scatter(packed[3], "fsdp", scatter_dimension=0, tiled=True),
        lax.psum_scatter(packed[4], "fsdp", scatter_dimension=0, tiled=True),
    )
    results = unpack_grads(shard_sums, owners)
    block_out = jnp.concatenate(out_blocks, axis=0)
    grad_tokens = jnp.concatenate(grad_blocks, axis=0)
    return (
        block_out,
        grad_tokens,
        results[0],
        results[1],
        results[2],
        results[3],
        results[4],
        results[5],
    )


def solution(mesh):
    in_specs = (
        P("fsdp", None),
        P("fsdp", None),
        P("fsdp", None),
        P("fsdp"),
        P("fsdp"),
        P("fsdp"),
        P("fsdp"),
        P("fsdp"),
        P("fsdp"),
    )
    out_specs = (
        P("fsdp", None),
        P("fsdp", None),
        P("fsdp"),
        P("fsdp"),
        P("fsdp"),
        P("fsdp"),
        P("fsdp"),
        P("fsdp"),
    )
    return jax.shard_map(shards, mesh=mesh, in_specs=in_specs, out_specs=out_specs, check_vma=False)
```

profile of v0, /device:TPU:0, one launch (start us, length us, event | category | flops | bytes accessed | tf_op | source)
XLA Modules:
  0.0 812.2 jit_solution(16830759048856803411)
XLA Ops:
  11.7 42.3 %all-reduce.8 = (bf16[7680]{0:T(1024)(128)(2,1)S(1)}, bf16[1536]{0:T(1024)(128)(2,1)S(1)}) all-reduce(bf16[7680]{0:T(1024)(128)(2,1)S(1)} %dynamic-update-slice.1, bf16[1536]{0:T(1024)(128)(2,1)S(1)} %dynamic-update-slice), channel_id=1, replica_groups=mesh['fsdp'=32] {'fsdp'}, use_global_device_ids=true, to_apply=%add.1 | all-reduce | flops 9216 | bytes 36864
  64.2 1.7 fusion.104
  65.9 1.8 fusion.77
  67.7 3.4 reshape.439
  71.1 58.5 %all-gather.5.cloned.1.call-done = bf16[1769472]{0:T(1024)(128)(2,1)} async-done(((bf16[55296]{0:T(1024)(128)(2,1)}), bf16[1769472]{0:T(1024)(128)(2,1)}) %all-gather.5.cloned.1.call-update) | async-done | bytes 3538960 | tf_op jit(solution)/shard_map/all_gather | solution.py:34
  129.6 6.3 reshape.435
  145.6 2.0 fusion.86
  147.6 1.8 reshape.442
  152.8 1.8 reshape.436
  157.5 1.8 fusion.149
  163.3 31.6 %all-gather.11.cloned.1.call-done = bf16[2359296]{0:T(1024)(128)(2,1)} async-done(((bf16[73728]{0:T(1024)(128)(2,1)}), bf16[2359296]{0:T(1024)(128)(2,1)}) %all-gather.11.cloned.1.call-update) | async-done | bytes 4718608 | tf_op jit(solution)/shard_map/all_gather | solution.py:37
  194.9 9.3 %reshape.441 = bf16[3072,768]{1,0:T(8,128)(2,1)} reshape(bf16[2359296]{0:T(1024)(128)(2,1)} %all-gather.11.cloned.1.call-done) | data formatting | bytes 9437184 | tf_op jit(solution)/shard_map/reshape | solution.py:50
  204.2 5.0 fusion.153
  209.2 2.4 fusion.154
  211.6 48.5 %all-gather.9.cloned.1.call-done = bf16[2359296]{0:T(1024)(128)(2,1)} async-done(((bf16[73728]{0:T(1024)(128)(2,1)}), bf16[2359296]{0:T(1024)(128)(2,1)}) %all-gather.9.cloned.1.call-update) | async-done | bytes 4718608 | tf_op jit(solution)/shard_map/all_gather | solution.py:36
  260.2 8.2 %reshape.440 = bf16[768,3072]{1,0:T(8,128)(2,1)} reshape(bf16[2359296]{0:T(1024)(128)(2,1)} %all-gather.9.cloned.1.call-done) | data formatting | bytes 9437184 | tf_op jit(solution)/shard_map/reshape | solution.py:49
  268.4 5.0 fusion.23
  275.0 2.3 fusion.19
  277.4 2.3 multiply_reduce_fusion.2
  286.4 2.0 convolution_convert_fusion.1
  289.5 1.8 fusion.6
  296.7 2.0 convolution_convert_fusion
  299.8 1.8 fusion.4
  302.6 2.0 fusion.92
  304.6 5.0 fusion.44
  311.3 1.8 copy.92
  313.1 1.7 reshape.446
  314.8 1.8 copy.96
  316.6 1.7 reshape.447
  320.0 1.8 copy.105
  321.8 1.7 reshape.450
  323.6 1.8 copy.109
  325.3 1.8 reshape.451
  327.1 2.9 reshape.455
  330.0 5.2 fusion.32
  335.2 6.6 reshape.453
  341.8 8.1 %reshape.457 = f32[32,73728]{1,0:T(8,128)} reshape(f32[768,3072]{1,0:T(8,128)} %fusion.44) | data formatting | bytes 18874368 | tf_op jit(solution)/shard_map/reshape | solution.py:111
  349.9 6.3 fusion.28
  356.2 8.1 reshape.459
  369.2 2.2 fusion.61
  386.7 41.6 %all-reduce.6 = f32[32,288]{1,0:T(8,128)S(1)} all-reduce(f32[32,288]{1,0:T(8,128)S(1)} %pad_maximum_fusion.8), channel_id=6, replica_groups=mesh['fsdp'=32] {'fsdp'}, use_global_device_ids=true, to_apply=%region_39.40.clone | all-reduce | flops 9216 | bytes 73728
  429.4 3.5 fusion.14
  433.1 3.6 fusion.15
  438.5 358.0 %all-reduce.11.cloned.1.call-done = (f32[32,55296]{1,0:T(8,128)}, f32[32,18432]{1,0:T(8,128)}, f32[32,73728]{1,0:T(8,128)}, f32[32,73728]{1,0:T(8,128)}) async-done(((f32[32,55296]{1,0:T(8,128)}, f32[32,18432]{1,0:T(8,128)}, f32[32,73728]{1,0:T(8,128)}, f32[32,73728]{1,0:T(8,128)}), (f32[32,55296]{1,0:T(8,128)}, f32[32,18432]{1,0:T(8,128)}, f32[32,73728]{1,0:T(8,128)}, ...) | async-done | bytes 28311568
  796.5 2.3 constant_dynamic-slice_fusion.4
  798.8 1.7 constant_dynamic-slice_fusion.3
  800.5 2.6 constant_dynamic-slice_fusion.2
  803.1 2.6 constant_dynamic-slice_fusion.1
  (305 shorter events, 74.5 us)
Async XLA Ops:
  7.2 60.5 %all-gather.7.cloned.1.call-start = ((), (), s32[]{:S(2)}) async-start(), calls=%async_computation.1 | async-start | bytes 1216512 | tf_op jit(solution)/shard_map/all_gather | solution.py:35
  7.9 121.7 %all-gather.5.cloned.1.call-start = ((), (), s32[]{:S(2)}) async-start(), calls=%async_computation | async-start | bytes 3649536 | tf_op jit(solution)/shard_map/all_gather | solution.py:34
  8.6 186.3 %all-gather.11.cloned.1.call-start = ((), (), s32[]{:S(2)}) async-start(), calls=%async_computation.3 | async-start | bytes 4866048 | tf_op jit(solution)/shard_map/all_gather | solution.py:37
  9.4 250.8 %all-gather.9.cloned.1.call-start = ((), (), s32[]{:S(2)}) async-start(), calls=%async_computation.2 | async-start | bytes 4866048 | tf_op jit(solution)/shard_map/all_gather | solution.py:36
  10.0 786.5 %all-reduce.11.cloned.1.call-start = ((), (), s32[]{:S(2)}) async-start(), calls=%async_computation.4 | async-start | bytes 56623104
  60.0 11.1 %copy-start.65 = (f32[64]{0:T(128)}, f32[64]{0:T(128)S(1)}, u32[]{:S(2)}) copy-start(f32[64]{0:T(128)S(1)} %get-tuple-element.92) | copy-start | bytes 772
  60.0 11.1 %copy-start.68 = (f32[64]{0:T(128)}, f32[64]{0:T(128)S(1)}, u32[]{:S(2)}) copy-start(f32[64]{0:T(128)S(1)} %get-tuple-element.91) | copy-start | bytes 772
  61.1 10.0 %copy-start.59 = (f32[64]{0:T(128)}, f32[64]{0:T(128)S(1)}, u32[]{:S(2)}) copy-start(f32[64]{0:T(128)S(1)} %get-tuple-element.90) | copy-start | bytes 772
  61.1 10.0 %copy-start.61 = (f32[64]{0:T(128)}, f32[64]{0:T(128)S(1)}, u32[]{:S(2)}) copy-start(f32[64]{0:T(128)S(1)} %get-tuple-element.89) | copy-start | bytes 772
  62.8 8.3 %copy-start.76 = (f32[64]{0:T(128)}, f32[64]{0:T(128)S(1)}, u32[]{:S(2)}) copy-start(f32[64]{0:T(128)S(1)} %fusion.128) | copy-start | bytes 772
  62.8 8.3 %copy-start.79 = (f32[64]{0:T(128)}, f32[64]{0:T(128)S(1)}, u32[]{:S(2)}) copy-start(f32[64]{0:T(128)S(1)} %fusion.130) | copy-start | bytes 772
  154.6 4.9 copy-start.27
  154.6 5.0 copy-start.29
  154.6 5.4 copy-start.44
  157.5 4.9 copy-start.55
  157.5 4.9 copy-start.63
  204.2 5.0 copy-start
  204.2 5.0 copy-start.39
  268.4 5.0 copy-start.1
  277.4 4.7 copy-start.3
  284.9 6.4 copy-start.30
  284.9 7.4 copy-start.4
  284.9 7.4 copy-start.42
  295.1 6.5 copy-start.28
  295.1 7.5 copy-start.41
  295.1 7.5 copy-start.43
  295.1 7.5 copy-start.46
  295.1 7.5 copy-start.48
  295.1 9.4 %copy-start.16 = (bf16[64,3072]{1,0:T(8,128)(2,1)S(1)}, bf16[64,3072]{1,0:T(8,128)(2,1)}, u32[]{:S(2)}) copy-start(bf16[64,3072]{1,0:T(8,128)(2,1)} %copy-done.15) | copy-start | bytes 1179652
  295.2 9.4 %copy-start.18 = (bf16[64,3072]{1,0:T(8,128)(2,1)S(1)}, bf16[64,3072]{1,0:T(8,128)(2,1)}, u32[]{:S(2)}) copy-start(bf16[64,3072]{1,0:T(8,128)(2,1)} %copy-done.17) | copy-start | bytes 1179652
  295.2 9.4 %copy-start.51 = (bf16[64,768]{1,0:T(8,128)(2,1)S(1)}, bf16[64,768]{1,0:T(8,128)(2,1)}, u32[]{:S(2)}) copy-start(bf16[64,768]{1,0:T(8,128)(2,1)} %get-tuple-element.62) | copy-start | bytes 294916
  295.2 9.4 %copy-start.52 = (bf16[64,768]{1,0:T(8,128)(2,1)S(1)}, bf16[64,768]{1,0:T(8,128)(2,1)}, u32[]{:S(2)}) copy-start(bf16[64,768]{1,0:T(8,128)(2,1)} %get-tuple-element.63) | copy-start | bytes 294916
  364.3 7.2 copy-start.54
  364.3 7.2 copy-start.60
  364.3 7.2 copy-start.62
  364.3 7.2 copy-start.8
  364.3 7.2 copy-start.36
  364.3 7.2 copy-start.37
  364.4 7.2 copy-start.38
  371.5 57.9 %copy-start.57 = (f32[768]{0:T(1024)S(1)}, f32[768]{0:T(1024)}, u32[]{:S(2)}) copy-start(f32[768]{0:T(1024)} %get-tuple-element.54) | copy-start | bytes 9220
  374.6 58.4 %copy-start.14 = (f32[64,768]{1,0:T(8,128)S(1)}, f32[64,768]{1,0:T(8,128)}, u32[]{:S(2)}) copy-start(f32[64,768]{1,0:T(8,128)} %copy-done.12) | copy-start | bytes 589828
  374.6 58.4 %copy-start.35 = (bf16[64,3072]{1,0:T(8,128)(2,1)S(1)}, bf16[64,3072]{1,0:T(8,128)(2,1)}, u32[]{:S(2)}) copy-start(bf16[64,3072]{1,0:T(8,128)(2,1)} %get-tuple-element.43) | copy-start | bytes 1179652
  374.6 58.4 %copy-start.70 = (f32[64]{0:T(128)S(1)}, f32[64]{0:T(128)}, u32[]{:S(2)}) copy-start(f32[64]{0:T(128)} %copy-done.68) | copy-start | bytes 772
  433.1 4.5 copy-start.24
  433.1 4.5 copy-start.34
  433.1 4.5 copy-start.67
  433.1 4.5 copy-start.78
  433.1 4.5 copy-start.87
  (55 other events, 137.9 us)
Sparse Core Ops, SparseCore 0:
  10.9 56.7 all-gather.6
  70.6 58.9 all-gather.4
  132.5 62.3 all-gather.10
  197.7 62.4 all-gather.8
  364.4 432.0 all-reduce.10
where the time goes:
time: 815 us; the launch traced here: 812 us
  waiting for transfers between devices  499 us (61%)
  local copies, waits for them, and re-layouts  117 us (14%)
  blocking collectives  83.9 us (10%)
  matrix products  71.2 us (9%)
  other arithmetic  23 us (3%)
  between operations  17.7 us (2%)
    unnamed x6, waiting for transfers between devices  361 us
    unnamed x2, blocking collectives  83.9 us
    all_gather x1, waiting for transfers between devices, fetch_params(): lax.all_gather(qkv_part, 'fsdp', axis=0, tiled=True)  58.5 us
    all_gather x1, waiting for transfers between devices, fetch_params(): lax.all_gather(up_part, 'fsdp', axis=0, tiled=True)  48.5 us
    all_gather x1, waiting for transfers between devices, fetch_params(): lax.all_gather(down_part, 'fsdp', axis=0, tiled=True)  31.6 us
    unnamed x209, local copies, waits for them, and re-layouts  21.7 us
  transfers between devices with their start and end apart: 5, of which 4 were waited for; matrix products, arithmetic and copies ran while one was open for 12% of the time, Pallas kernels for 0%

commit v1 on v0

v1 whole, which is shorter than its diff:
```python
import functools

import jax
import jax.numpy as jnp
from jax import lax
from jax.experimental import pallas as pl
from jax.experimental.pallas import tpu as pltpu
from jax.sharding import PartitionSpec as P

D = 768
H = 12
HD = 64
FF = 3072
ROWS = 64
EPSILON = 1e-05
NEGATIVE = -1e30
MESH = pl.DeviceIdType.MESH
SHAPES = ((D, 3 * D), (D, D), (D, FF), (FF, D))
SMALL = 2 * D + 6 * D + FF
HALVES = ((0, 1, 2), (0, 2, 1))


def grid_of(devices):
    known = {32: (4, 2, 2), 256: (4, 4, 8)}
    return known.get(devices, (devices // 8, 2, 2)) + (2,)


def slab_of(rows, cols, devices):
    if rows % devices == 0 and (rows // devices) % 8 == 0:
        return rows // devices, cols
    return rows * cols // devices // 256, 256


def slabs_of(devices):
    return [slab_of(r, c, devices) for r, c in SHAPES] + [(16, 256)]


def place(dims):
    me = lax.axis_index("fsdp")
    strides = [1] * 4
    for d in (2, 1, 0):
        strides[d] = strides[d + 1] * dims[d + 1]
    at = [lax.rem(me // strides[d], dims[d]) for d in range(4)]

    def other(d, step):
        digit = lax.rem(at[d] + step, dims[d])
        return digit, me + (digit - at[d]) * strides[d]

    return at, other


def greet(dims, other):
    barrier = pltpu.get_barrier_semaphore()
    count = 0
    for d in range(4):
        for step in range(1, dims[d]):
            pl.semaphore_signal(barrier, inc=1, device_id=(other(d, step)[1],), device_id_type=MESH)
            count += 1
    pl.semaphore_wait(barrier, count)


def half_cols(ref, half):
    width = ref.shape[-1] // 2
    return pl.ds(half * width, width)


def gather_kernel(dims, n, *refs):
    ins, outs = refs[:n], refs[n : 2 * n]
    local_sem, send_sem, recv_sem = refs[2 * n :]
    at, other = place(dims)
    greet(dims, other)
    locals_ = []
    for a in range(n):
        copy = pltpu.make_async_copy(ins[a], outs[a].at[at[0], at[1], at[2], at[3]], local_sem.at[a])
        copy.start()
        locals_.append(copy)

    def send(a, half, phase):
        cols = half_cols(outs[a], half)
        order = HALVES[half]
        dim = order[phase]
        where = [slice(None) if d in order[:phase] else at[d] for d in range(4)]
        base = sum(dims[d] - 1 for d in order[:phase])
        copies = []
        for step in range(1, dims[dim]):
            target = outs[a].at[tuple(where) + (slice(None), cols)]
            source = ins[a].at[:, cols] if phase == 0 else target
            sem = (a, half, base + step - 1)
            copy = pltpu.make_async_remote_copy(
                source,
                target,
                send_sem.at[sem],
                recv_sem.at[sem],
                device_id=(other(dim, step)[1],),
                device_id_type=MESH,
            )
            copy.start()
            copies.append(copy)
        return copies

    last = sum(dims[:3]) - 3
    flying, cores = {}, {}

    def advance(a, phase):
        if phase == 1:
            locals_[a].wait()
        if phase <= 2:
            for half in range(2):
                if phase:
                    for copy in flying[a, half, phase - 1]:
                        copy.wait_recv()
                flying[a, half, phase] = send(a, half, phase)
        elif phase == 3:
            for half in range(2):
                for copy in flying[a, half, 2]:
                    copy.wait_recv()
            block = outs[a].at[:, :, :, at[3]]
            sem = (a, 0, last)
            cores[a] = pltpu.make_async_remote_copy(
                block, block, send_sem.at[sem], recv_sem.at[sem],
                device_id=(other(3, 1)[1],), device_id_type=MESH,
            )
            cores[a].start()
        else:
            cores[a].wait_recv()

    for a in range(n):
        advance(a, 0)
    for t in range(n + 3):
        for phase in range(1, 5):
            a = t - phase + 1
            if 0 <= a < n:
                advance(a, phase)
    for copies in flying.values():
        for copy in copies:
            copy.wait_send()
    for copy in cores.values():
        copy.wait_send()


def gather(parts, dims):
    n = len(parts)
    steps = sum(dims[:3]) - 2
    return pl.pallas_call(
        functools.partial(gather_kernel, dims, n),
        out_shape=[jax.ShapeDtypeStruct(dims + p.shape, p.dtype) for p in parts],
        in_specs=[pl.BlockSpec(memory_space=pl.ANY)] * n,
        out_specs=[pl.BlockSpec(memory_space=pl.ANY)] * n,
        scratch_shapes=[
            pltpu.SemaphoreType.DMA((n,)),
            pltpu.SemaphoreType.DMA((n, 2, steps)),
            pltpu.SemaphoreType.DMA((n, 2, steps)),
        ],
        compiler_params=pltpu.CompilerParams(collective_id=0, has_side_effects=True),
    )(*parts)


def add_blocks(total, terms, lead):
    count = 1
    for size in lead:
        count *= size

    def body(flat, carry):
        where, rest = [], flat
        for size in reversed(lead):
            where.insert(0, lax.rem(rest, size))
            rest = rest // size
        value = terms[0](where)[...].astype(jnp.float32)
        for term in terms[1:]:
            value = value + term(where)[...].astype(jnp.float32)
        out = total(where)
        out[...] = value.astype(out.dtype)
        return carry

    if count == 1:
        body(0, 0)
    else:
        lax.fori_loop(0, count, body, 0)


def reduce_scratch(dims, slab):
    rows, cols = slab
    shapes = [dims[:3] + slab]
    for half in range(2):
        left = [0, 1, 2]
        for dim in reversed(HALVES[half]):
            left.remove(dim)
            shapes.append((dims[dim] - 1,) + tuple(dims[d] for d in left) + (rows, cols // 2))
    return shapes


def reduce_kernel(dims, n, *refs):
    ins, outs = refs[:n], refs[n : 2 * n]
    scratch = [refs[2 * n + 7 * a : 2 * n + 7 * a + 7] for a in range(n)]
    send_sem, recv_sem = refs[9 * n :]
    at, other = place(dims)
    greet(dims, other)
    last = sum(dims[:3]) - 3
    flying = {}

    def remote(src, dst, sem, device):
        copy = pltpu.make_async_remote_copy(
            src, dst, send_sem.at[sem], recv_sem.at[sem], device_id=(device,), device_id_type=MESH
        )
        copy.start()
        return copy

    def held(a, half, phase):
        if phase == 0:
            return scratch[a][0], [0, 1, 2], half_cols(scratch[a][0], half)
        left = list(HALVES[half][: 3 - phase])
        return scratch[a][3 * half + phase].at[0], sorted(left), slice(None)

    def push(a, half, phase):
        ref, lead, cols = held(a, half, phase - 1)
        dim = HALVES[half][3 - phase]
        base = sum(dims[d] - 1 for d in HALVES[half][4 - phase :])
        copies = []
        for step in range(1, dims[dim]):
            digit, device = other(dim, step)
            where = tuple(digit if d == dim else slice(None) for d in lead)
            copies.append(
                remote(
                    ref.at[where + (slice(None), cols)],
                    scratch[a][3 * half + phase].at[step - 1],
                    (a, half, base + step - 1),
                    device,
                )
            )
        flying[a, half, phase] = copies

    def absorb(a, half, phase):
        for copy in flying[a, half, phase]:
            copy.wait_recv()
        ref, lead, cols = held(a, half, phase - 1)
        dim = HALVES[half][3 - phase]
        left = [d for d in lead if d != dim]
        landed = scratch[a][3 * half + phase]

        def own(where):
            place_of = dict(zip(left, where))
            return ref.at[tuple(at[d] if d == dim else place_of[d] for d in lead) + (slice(None), cols)]

        terms = [own] + [
            (lambda where, s=s: landed.at[(s,) + tuple(where)]) for s in range(dims[dim] - 1)
        ]
        if phase == 3:
            total = lambda where: outs[a].at[:, half_cols(outs[a], half)]
        else:
            total = lambda where: landed.at[(0,) + tuple(where)]
        add_blocks(total, terms, [dims[d] for d in left])

    def advance(a, phase):
        if phase == 0:
            flying[a, 0, 0] = [
                remote(ins[a].at[:, :, :, 1 - at[3]], scratch[a][0], (a, 0, last), other(3, 1)[1])
            ]
            return
        if phase == 1:
            for copy in flying[a, 0, 0]:
                copy.wait_recv()
            add_blocks(
                lambda w: scratch[a][0].at[tuple(w)],
                [lambda w: ins[a].at[tuple(w) + (at[3],)], lambda w: scratch[a][0].at[tuple(w)]],
                list(dims[:3]),
            )
        for half in range(2):
            if phase > 1:
                absorb(a, half, phase - 1)
            if phase < 4:
                push(a, half, phase)

    for a in range(n):
        advance(a, 0)
    for t in range(n + 3):
        for phase in range(1, 5):
            a = t - phase + 1
            if 0 <= a < n:
                advance(a, phase)
    for copies in flying.values():
        for copy in copies:
            copy.wait_send()


def reduce_scatter(parts, dims):
    n = len(parts)
    steps = sum(dims[:3]) - 2
    scratch = []
    for p in parts:
        scratch += [pltpu.VMEM(s, p.dtype) for s in reduce_scratch(dims, p.shape[4:])]
    return pl.pallas_call(
        functools.partial(reduce_kernel, dims, n),
        out_shape=[jax.ShapeDtypeStruct(p.shape[4:], jnp.float32) for p in parts],
        in_specs=[pl.BlockSpec(memory_space=pltpu.VMEM)] * n,
        out_specs=[pl.BlockSpec(memory_space=pltpu.VMEM)] * n,
        scratch_shapes=scratch
        + [
            pltpu.SemaphoreType.DMA((n, 2, steps)),
            pltpu.SemaphoreType.DMA((n, 2, steps)),
        ],
        compiler_params=pltpu.CompilerParams(
            collective_id=1, has_side_effects=True, vmem_limit_bytes=60 * 2**20
        ),
    )(*parts)


def norm_forward(values, gain, shift):
    center = values - jnp.mean(values, axis=-1, keepdims=True)
    scale = lax.rsqrt(jnp.mean(center * center, axis=-1, keepdims=True) + EPSILON)
    normal = center * scale
    return normal * gain + shift, normal, scale


def norm_backward(grad, normal, scale, gain):
    e = grad * gain
    back = scale * (
        e
        - jnp.mean(e, axis=-1, keepdims=True)
        - normal * jnp.mean(e * normal, axis=-1, keepdims=True)
    )
    return back, jnp.sum(grad * normal, axis=0), jnp.sum(grad, axis=0)


def low(values):
    return values.astype(jnp.bfloat16)


def dot(a, b, dims):
    return lax.dot_general(a, b, (dims, ((), ())), preferred_element_type=jnp.float32)


NN = ((1,), (0,))
NT = ((1,), (1,))
TN = ((0,), (0,))


def masks(lengths, rows):
    position = jnp.arange(rows, dtype=jnp.int32)
    local = position % ROWS
    batch = position // ROWS
    first = jnp.repeat(lengths[:, 0], ROWS)
    end = first + jnp.repeat(lengths[:, 1], ROWS)
    segment = (local >= first).astype(jnp.int32) + (local >= end).astype(jnp.int32) + 3 * batch
    allowed = (position[None, :] <= position[:, None]) & (segment[None, :] == segment[:, None])
    return allowed, (local < end).astype(jnp.float32)[:, None]


def block(tokens, lengths, cotangent, weights, gains, shifts, up_bias):
    w_qkv, w_out, w_up, w_down = weights
    rows = tokens.shape[0]
    scale = HD ** (-0.5)
    allowed, live = masks(lengths, rows)
    x = tokens.astype(jnp.float32)
    h1, normal1, scale1 = norm_forward(x, gains[0], shifts[0])
    h1 = low(h1)
    mixed = dot(h1, w_qkv, NN)
    q = low(mixed[:, :D] + shifts[2]).reshape(rows, H, HD).transpose(1, 0, 2)
    k = low(mixed[:, D : 2 * D]).reshape(rows, H, HD).transpose(1, 0, 2)
    v = low(mixed[:, 2 * D :] + shifts[3]).reshape(rows, H, HD).transpose(1, 0, 2)

    def bmm(spec, a, b):
        return jnp.einsum(spec, a, b, preferred_element_type=jnp.float32)

    s = jnp.where(allowed, bmm("hqe,hke->hqk", q, k) * scale, NEGATIVE)
    p = jnp.exp(s - jnp.max(s, axis=-1, keepdims=True))
    p = p / jnp.sum(p, axis=-1, keepdims=True)
    pb = low(p)
    o = low(bmm("hqk,hke->hqe", pb, v)).transpose(1, 0, 2).reshape(rows, D)
    y1 = x + dot(o, w_out, NN) + shifts[4]
    h2, normal2, scale2 = norm_forward(y1, gains[1], shifts[1])
    h2 = low(h2)
    u = dot(h2, w_up, NN) + up_bias
    t = jnp.tanh(0.7978845608028654 * (u + 0.044715 * u * u * u))
    z = low(0.5 * u * (1.0 + t))
    slope = 0.5 * (1.0 + t) + 0.5 * u * (1.0 - t * t) * 0.7978845608028654 * (
        1.0 + 3 * 0.044715 * u * u
    )
    out = low(live * (y1 + dot(z, w_down, NN) + shifts[5]))
    dy = live * cotangent.astype(jnp.float32)
    dyl = low(dy)
    du = low(dot(dyl, w_down, NT) * slope)
    g_down = low(dot(z, dyl, TN))
    dh2 = dot(du, w_up, NT)
    g_up = low(dot(h2, du, TN))
    back, gain2, shift2 = norm_backward(dh2, normal2, scale2, gains[1])
    dy1 = dy + back
    da = low(dy1)
    do = low(dot(da, w_out, NT)).reshape(rows, H, HD).transpose(1, 0, 2)
    g_out = low(dot(o, da, TN))
    dp = bmm("hqe,hke->hqk", do, v)
    dv = low(bmm("hqk,hqe->hke", pb, do))
    ds = low(p * (dp - jnp.sum(p * dp, axis=-1, keepdims=True)))
    dq = low(bmm("hqk,hke->hqe", ds, k) * scale)
    dk = low(bmm("hqk,hqe->hke", ds, q) * scale)
    dmixed = jnp.concatenate(
        [a.transpose(1, 0, 2).reshape(rows, D) for a in (dq, dk, dv)], axis=1
    )
    g_qkv = low(dot(h1, dmixed, TN))
    dh1 = dot(dmixed, w_qkv, NT)
    back, gain1, shift1 = norm_backward(dh1, normal1, scale1, gains[0])
    grad_tokens = low(dy1 + back)
    f32 = lambda a: jnp.sum(a.astype(jnp.float32), axis=0)
    sums = jnp.concatenate(
        [shift1, shift2, f32(dmixed[:, :D]), f32(dmixed[:, 2 * D :]), f32(da), f32(dyl), f32(du)]
    )
    return out, grad_tokens, (g_qkv, g_out, g_up, g_down), jnp.concatenate([gain1, gain2]), sums


def shards(dims, tokens, lengths, cotangent, w_qkv, w_out, w_up, w_down, gains, biases):
    devices = dims[0] * dims[1] * dims[2] * dims[3]
    slabs = slabs_of(devices)
    own_gain, own_bias = gains.shape[0], biases.shape[0]
    small = jnp.concatenate([gains, biases])
    small = jnp.pad(small, (0, 4096 - own_gain - own_bias))
    parts = [p.reshape(s) for p, s in zip((w_qkv, w_out, w_up, w_down, small), slabs)]
    order = (4, 0, 1, 2, 3)
    got = gather([parts[i] for i in order], dims)
    got = [got[order.index(i)] for i in range(5)]
    weights = [g.reshape(shape) for g, shape in zip(got[:4], SHAPES)]
    small = got[4].reshape(devices, 4096)
    gain_all = small[:, :own_gain].reshape(2, D).astype(jnp.float32)
    bias_all = small[:, own_gain : own_gain + own_bias].reshape(-1).astype(jnp.float32)
    out, grad_tokens, grads, gain_sums, bias_sums = block(
        tokens, lengths, cotangent, weights, gain_all, bias_all[: 6 * D].reshape(6, D), bias_all[6 * D :]
    )
    small = jnp.concatenate(
        [gain_sums.reshape(devices, own_gain), bias_sums.reshape(devices, own_bias)], axis=1
    )
    small = low(jnp.pad(small, ((0, 0), (0, 4096 - own_gain - own_bias))))
    parts = [g.reshape(dims + s) for g, s in zip(tuple(grads) + (small,), slabs)]
    order = (3, 2, 0, 1, 4)
    sums = reduce_scatter([parts[i] for i in order], dims)
    sums = [sums[order.index(i)] for i in range(5)]
    small = sums[4].reshape(-1)
    return (
        out,
        grad_tokens,
        *[g.reshape(-1) for g in sums[:4]],
        small[:own_gain],
        small[own_gain : own_gain + own_bias],
    )


def solution(mesh):
    rows, flat = P("fsdp", None), P("fsdp")
    return jax.shard_map(
        functools.partial(shards, grid_of(mesh.shape["fsdp"])),
        mesh=mesh,
        in_specs=(rows,) * 3 + (flat,) * 6,
        out_specs=(rows,) * 2 + (flat,) * 6,
        check_vma=False,
    )
```

time: 815 us -> 251 us (0.31)
  waiting for transfers between devices: 499 us -> 0 us
  Pallas kernels: 0 us -> 182 us
  local copies, waits for them, and re-layouts: 117 us -> 23.2 us
  blocking collectives: 83.9 us -> 0 us
  matrix products: 71.2 us -> 41.1 us
  other arithmetic: 23 us -> 3.45 us
  between operations: 17.7 us -> 1.13 us
    unnamed x6 -> x0, waiting for transfers between devices: 361 us -> none
    pallas_call x0 -> x2, Pallas kernels: none -> 182 us  [the longest x1 96.6 us: reduce_scatter(): pl.pallas_call(functools.partial(reduce_kernel, dims, n), out_shape=[jax....]
    all_gather x4 -> x0, waiting for transfers between devices: 139 us -> none  [the longest x1 58.5 us: fetch_params(): lax.all_gather(qkv_part, 'fsdp', axis=0, tiled=True)]
    unnamed x2 -> x0, blocking collectives: 83.9 us -> none
    reshape x31 -> x11, local copies, waits for them, and re-layouts: 81.1 us -> 12.2 us  [the longest x5 7.08 us: shards(): p.reshape(s)]
    dot_general x32 -> x17, matrix products: 71.2 us -> 39.8 us  [the longest x12 33 us: dot(): lax.dot_general(a, b, (dims, ((), ())), preferred_element_type=jnp.float32)]
    unnamed x209 -> x90, local copies, waits for them, and re-layouts: 21.7 us -> 6.47 us
    convert_element_type x10 -> x6, other arithmetic: 9.64 us -> 1.14 us  [the longest x3 1.06 us: low(): return values.astype(jnp.bfloat16)]
  transfers between devices with their start and end apart: 5 -> 0, of which waited for: 4 -> 0; matrix products, arithmetic and copies ran while one was open for 12% -> 0% of each run, Pallas kernels for 0% -> 0%
where the time goes in v1:
time: 251 us
  Pallas kernels  182 us (73%)
  matrix products  41.1 us (16%)
  local copies, waits for them, and re-layouts  23.2 us (9%)
  other arithmetic  3.45 us (1%)
    pallas_call x1, Pallas kernels, reduce_scatter(): pl.pallas_call(functools.partial(reduce_kernel, dims, n), out_shape=[jax....  96.6 us
    pallas_call x1, Pallas kernels, gather(): pl.pallas_call(functools.partial(gather_kernel, dims, n), out_shape=[jax....  85.3 us
    dot_general x12, matrix products, dot(): lax.dot_general(a, b, (dims, ((), ())), preferred_element_type=jnp.float32)  33 us
    reshape x5, local copies, waits for them, and re-layouts, shards(): p.reshape(s)  7.08 us
    dot_general x5, matrix products, bmm(): return jnp.einsum(spec, a, b, preferred_element_type=jnp.float32)  6.73 us
    unnamed x90, local copies, waits for them, and re-layouts  6.47 us

profile of v1, /device:TPU:0, one launch (start us, length us, event | category | flops | bytes accessed | tf_op | source)
XLA Modules:
  0.0 250.8 jit_solution(12639932334849378708)
XLA Ops:
  0.6 0.8 fusion.45
  1.4 0.6 reshape.276.refs_0_
  2.0 1.7 reshape.277.refs_1_
  3.7 1.4 reshape.278.refs_2_
  5.2 1.6 reshape.279.refs_3_
  6.8 1.7 reshape.280.refs_4_
  8.5 85.3 %shard_map.152 = (bf16[4,2,2,2,16,256]{5,4,3,2,1,0:T(8,128)(2,1)}, bf16[4,2,2,2,24,2304]{5,4,3,2,1,0:T(8,128)(2,1)}, bf16[4,2,2,2,24,768]{5,4,3,2,1,0:T(8,128)(2...) custom-call(bf16[16,256]{1,0:T(8,128)(2,1)} %reshape.276.refs_0_, ...), custom_call_target="tpu_custom_call" | custom-call | tf_op jit(solution)/shard_map/pallas_call | solution.py:144
  93.8 1.0 copy.37
  95.3 0.2 fusion.33
  95.5 2.7 %fusion.60 = f32[128,2304]{1,0:T(8,128)S(1)} fusion(bf16[768,2304]{1,0:T(8,128)(2,1)} %bitcast.80, bf16[128,768]{1,0:T(8,128)(2,1)S(1)} %copy-done, f32[768]{0:T(1024)S(1)} %get-tuple-element.48, f32[768]{0:T(1024)S(1)} %mul.199, f32[128]{0:T(128)S(1)} %add_rsqrt_fusion.1, f32[128]{0:T(128)S(1)} %broadcast_multiply_fusion.5), kind=kOutput, calls=%fused_computation.118 | convolution fusion | flops 453574656 | bytes 4922368 | tf_op jit(solution)/shard_map/dot_general | solution.py:329
  98.9 0.2 slice_reduce_fusion
  99.5 1.3 fusion.64
  100.8 0.6 convolution_convert_fusion.4
  101.5 0.6 copy-done.1
  102.1 0.4 fusion.65
  102.7 0.2 multiply_reduce_fusion.3
  102.9 3.2 %convolution_add_fusion = f32[128,3072]{1,0:T(8,128)S(1)} fusion(bf16[768,3072]{1,0:T(8,128)(2,1)} %bitcast.73, f32[3072]{0:T(1024)S(1)} %slice.102, f32[128,768]{1,0:T(8,128)S(1)} %get-tuple-element.54, f32[768]{0:T(1024)S(1)} %get-tuple-element.43, f32[768]{0:T(1024)S(1)} %mul.207, f32[128]{0:T(128)S(1)} %add_rsqrt_fusion, f32[128]{0:T(128)S(1)} %broadcast_multiply_fusion.4), kind=kOutput, calls=%fused_computation.5 | convolution fusion | flops 604864512 | bytes 6704128 | tf_op jit(solution)/shard_map/dot_general | solution.py:329
  106.1 4.2 %fusion.13 = bf16[128,768]{1,0:T(8,128)(2,1)} fusion(f32[128,768]{1,0:T(8,128)S(1)} %get-tuple-element.54, bf16[3072,768]{1,0:T(8,128)(2,1)} %bitcast.112, f32[768]{0:T(1024)S(1)} %get-tuple-element.44, f32[128]{0:T(128)S(1)} %compare_convert_fusion.2, f32[128,3072]{1,0:T(8,128)S(1)} %convolution_add_fusion), kind=kOutput, calls=%fused_computation.27 | convolution fusion | flops 607911936 | bytes 6884864 | tf_op jit(solution)/shard_map/dot_general | solution.py:329
  110.3 4.8 %fusion.66 = (bf16[3072]{0:T(1024)(128)(2,1)}, bf16[128,3072]{1,0:T(8,128)(2,1)S(1)}) fusion(f32[128,3072]{1,0:T(8,128)S(1)} %convolution_add_fusion, bf16[3072,768]{1,0:T(8,128)(2,1)} %bitcast.113, bf16[128,768]{1,0:T(8,128)(2,1)S(1)} %copy-done.9, f32[128]{0:T(128)S(1)} %compare_convert_fusion.2), kind=kOutput, calls=%fused_computation.123 | convolution fusion | flops 612135936 | bytes 7281152 | tf_op jit(solution)/shard_map/dot_general | solution.py:329
  115.2 2.3 multiply_reduce_fusion.1
  117.5 0.8 convert_reduce_fusion.1
  118.3 0.4 copy-done.2
  118.8 1.2 convolution_convert_fusion.6
  120.0 1.7 copy.29
  121.7 3.1 %bitcast_reduce_fusion = (bf16[12,64]{1,0:T(8,128)(2,1)}, bf16[12,128,64]{1,2,0:T(8,128)(2,1)}) fusion(bf16[12,128,64]{1,2,0:T(8,128)(2,1)} %bitcast.107, f32[12,128]{1,0:T(8,128)} %copy-done.22, bf16[12,128,64]{1,2,0:T(8,128)(2,1)} %bitcast.92, bf16[12,128,64]{1,2,0:T(8,128)(2,1)} %bitcast.96, pred[128,128]{0,1:T(8,128)(4,1)} %copy-done.16), kind=kOutput, calls=%fused_computation.76 | convolution fusion | flops 51512192 | bytes 810496 | tf_op jit(solution)/shard_map/hqk,hqe->hke/dot_general | solution.py:362
  124.8 1.8 multiply_reduce_fusion
  126.8 0.4 fusion.14
  127.2 0.9 bitcast_reduce_fusion.1
  128.1 0.5 copy-done.3
  128.6 1.9 fusion.32
  130.6 0.9 fusion.31
  131.5 4.0 %convolution_convert_fusion.2 = bf16[3072,768]{1,0:T(8,128)(2,1)} fusion(bf16[128,768]{1,0:T(8,128)(2,1)S(1)} %copy-done.10, f32[128]{0:T(128)S(1)} %copy-done.35, f32[128,3072]{1,0:T(8,128)S(1)} %convolution_add_fusion), kind=kOutput, calls=%fused_computation.3 | convolution fusion | flops 610172928 | bytes 6488576 | tf_op jit(solution)/shard_map/dot_general | solution.py:329
  135.5 3.7 %convolution_convert_fusion.1 = bf16[768,3072]{1,0:T(8,128)(2,1)} fusion(bf16[128,3072]{1,0:T(8,128)(2,1)S(1)} %get-tuple-element.64, f32[128,768]{1,0:T(8,128)S(1)} %get-tuple-element.54, f32[768]{0:T(1024)S(1)} %get-tuple-element.43, f32[768]{0:T(1024)S(1)} %mul.207, f32[128]{0:T(128)S(1)} %copy-done.19, f32[128]{0:T(128)S(1)} %copy-done.14), kind=kOutput, calls=%fused_computation.2 | convolution fusion | flops 606830592 | bytes 5905408 | tf_op jit(solution)/shard_map/dot_general | solution.py:329
  139.1 3.0 %convolution_convert_fusion = bf16[768,2304]{1,0:T(8,128)(2,1)} fusion(bf16[128,768]{0,1:T(8,128)(2,1)S(1)} %bitcast.104, bf16[128,768]{0,1:T(8,128)(2,1)S(1)} %bitcast.85, bf16[128,768]{0,1:T(8,128)(2,1)S(1)} %bitcast.87, bf16[128,768]{1,0:T(8,128)(2,1)S(1)} %copy-done, f32[768]{0:T(1024)S(1)} %get-tuple-element.48, f32[768]{0:T(1024)S(1)} %mul.199, ...), kind=kOutput, calls=%fused_computation.1 | convolution fusion | flops 457113600 | bytes 4332544 | tf_op jit(solution)/shard_map/dot_general | solution.py:329
  142.2 1.5 convolution_convert_fusion.3
  143.9 0.2 dynamic-update-slice.1
  144.2 0.2 dynamic-update-slice.2
  144.6 0.2 dynamic-update-slice.4
  144.8 0.2 dynamic-update-slice.5
  145.1 0.3 dynamic-update-slice.6
  145.7 0.8 copy.38
  146.4 96.6 %shard_map.153 = (f32[96,768]{1,0:T(8,128)}, f32[24,3072]{1,0:T(8,128)}, f32[24,2304]{1,0:T(8,128)}, f32[24,768]{1,0:T(8,128)}, f32[16,256]{1,0:T(8,128)}) custom-call(bf16[4,2,2,2,96,768]{5,4,3,2,1,0:T(8,128)(2,1)} %bitcast.70, bf16[4,2,2,2,24,3072]{5,4,3,2,1,0:T(8,128)(2,1)} %bitcast.71, bf16[4,2,2,2,24,2304]{5,4,3,2,1,0:T(8,128)(2,1)} %bitcast.72, ...), custom_call_target="tpu_custom_call" | custom-call | tf_op jit(solution)/shard_map/pallas_call | solution.py:291
  243.1 1.6 reshape.300
  244.7 1.5 reshape.301
  246.2 1.7 copy.39
  248.0 1.7 reshape.303
  249.7 0.5 slice.104
  250.2 0.6 slice.105
  (117 shorter events, 2.7 us)
Async XLA Ops:
  0.6 94.5 %copy-start = (bf16[128,768]{1,0:T(8,128)(2,1)S(1)}, bf16[128,768]{1,0:T(8,128)(2,1)}, u32[]{:S(2)}) copy-start(bf16[128,768]{1,0:T(8,128)(2,1)} %param.9) | copy-start | bytes 589828
  95.3 2.9 %copy-start.20 = (f32[128]{0:T(128)}, f32[128]{0:T(128)S(1)}, u32[]{:S(2)}) copy-start(f32[128]{0:T(128)S(1)} %broadcast_multiply_fusion.5) | copy-start | bytes 1540
  95.5 2.7 %copy-start.28 = (f32[128]{0:T(128)}, f32[128]{0:T(128)S(1)}, u32[]{:S(2)}) copy-start(f32[128]{0:T(128)S(1)} %add_rsqrt_fusion.1) | copy-start | bytes 1540
  98.2 0.7 copy-start.32
  98.5 3.0 %copy-start.12 = (bf16[128,768]{0,1:T(8,128)(2,1)}, bf16[128,768]{0,1:T(8,128)(2,1)S(1)}, u32[]{:S(2)}) copy-start(bf16[128,768]{0,1:T(8,128)(2,1)S(1)} %copy.27) | copy-start | bytes 589828
  98.6 2.8 %copy-start.4 = (bf16[128,768]{0,1:T(8,128)(2,1)}, bf16[128,768]{0,1:T(8,128)(2,1)S(1)}, u32[]{:S(2)}) copy-start(bf16[128,768]{0,1:T(8,128)(2,1)S(1)} %copy.25) | copy-start | bytes 589828
  98.8 2.6 %copy-start.6 = (bf16[128,768]{0,1:T(8,128)(2,1)}, bf16[128,768]{0,1:T(8,128)(2,1)S(1)}, u32[]{:S(2)}) copy-start(bf16[128,768]{0,1:T(8,128)(2,1)S(1)} %copy.26) | copy-start | bytes 589828
  99.5 2.0 copy-start.16
  100.8 0.7 copy-start.22
  100.8 1.3 copy-start.1
  102.6 7.8 %copy-start.33 = (f32[128]{0:T(128)}, f32[128]{0:T(128)S(1)}, u32[]{:S(2)}) copy-start(f32[128]{0:T(128)S(1)} %compare_convert_fusion.2) | copy-start | bytes 1540
  102.7 14.8 %copy-start.13 = (f32[128]{0:T(128)}, f32[128]{0:T(128)S(1)}, u32[]{:S(2)}) copy-start(f32[128]{0:T(128)S(1)} %broadcast_multiply_fusion.4) | copy-start | bytes 1540
  102.9 14.6 %copy-start.18 = (f32[128]{0:T(128)}, f32[128]{0:T(128)S(1)}, u32[]{:S(2)}) copy-start(f32[128]{0:T(128)S(1)} %add_rsqrt_fusion) | copy-start | bytes 1540
  106.1 4.2 %copy-start.9 = (bf16[128,768]{1,0:T(8,128)(2,1)S(1)}, bf16[128,768]{1,0:T(8,128)(2,1)}, u32[]{:S(2)}) copy-start(bf16[128,768]{1,0:T(8,128)(2,1)} %param.11) | copy-start | bytes 589828
  106.1 9.1 %slice-start = ((s8[4718592]{0:T(1024)(128)(4,1)}), s8[4194304]{0:T(1024)(128)(4,1)S(1)}, s32[]{:S(2)}) async-start(s8[4718592]{0:T(1024)(128)(4,1)} %bitcast.74), calls=%async_computation | async-start | bytes 8388608
  110.3 4.8 %slice-start.1 = ((s8[4718592]{0:T(1024)(128)(4,1)}), s8[524288]{0:T(1024)(128)(4,1)S(1)}, s32[]{:S(2)}) async-start(s8[4718592]{0:T(1024)(128)(4,1)} %bitcast.74), calls=%async_computation.1 | async-start | bytes 1048576
  115.2 2.3 copy-start.34
  117.5 1.3 copy-start.2
  124.8 1.8 copy-start.8
  124.8 1.8 copy-start.23
  124.8 2.0 copy-start.5
  124.8 2.4 copy-start.7
  124.8 3.3 %copy-start.11 = (bf16[12,128,64]{1,2,0:T(8,128)(2,1)S(1)}, bf16[12,128,64]{1,2,0:T(8,128)(2,1)}, u32[]{:S(2)}) copy-start(bf16[12,128,64]{1,2,0:T(8,128)(2,1)} %get-tuple-element.62) | copy-start | bytes 589828
  126.6 2.0 copy-start.3
  126.6 2.0 copy-start.21
  126.6 2.0 copy-start.29
  128.6 2.8 %copy-start.10 = (bf16[128,768]{1,0:T(8,128)(2,1)S(1)}, bf16[128,768]{1,0:T(8,128)(2,1)}, u32[]{:S(2)}) copy-start(bf16[128,768]{1,0:T(8,128)(2,1)} %param.11) | copy-start | bytes 589828
  128.6 2.8 %copy-start.35 = (f32[128]{0:T(128)S(1)}, f32[128]{0:T(128)}, u32[]{:S(2)}) copy-start(f32[128]{0:T(128)} %copy-done.33) | copy-start | bytes 1540
  131.5 4.0 %copy-start.14 = (f32[128]{0:T(128)S(1)}, f32[128]{0:T(128)}, u32[]{:S(2)}) copy-start(f32[128]{0:T(128)} %copy-done.13) | copy-start | bytes 1540
  131.5 4.0 %copy-start.19 = (f32[128]{0:T(128)S(1)}, f32[128]{0:T(128)}, u32[]{:S(2)}) copy-start(f32[128]{0:T(128)} %copy-done.18) | copy-start | bytes 1540
  142.1 1.6 copy-start.37
  142.2 1.7 copy-start.27
  142.2 2.0 copy-start.15
  142.2 2.2 copy-start.31
  142.2 2.5 copy-start.26
  142.2 2.7 %copy-start.25 = (bf16[768]{0:T(1024)(128)(2,1)S(1)}, bf16[768]{0:T(1024)(128)(2,1)}, u32[]{:S(2)}) copy-start(bf16[768]{0:T(1024)(128)(2,1)} %get-tuple-element.42) | copy-start | bytes 4612
  142.2 2.9 %copy-start.30 = (bf16[3072]{0:T(1024)(128)(2,1)S(1)}, bf16[3072]{0:T(1024)(128)(2,1)}, u32[]{:S(2)}) copy-start(bf16[3072]{0:T(1024)(128)(2,1)} %get-tuple-element.63) | copy-start | bytes 18436
  142.2 3.2 %copy-start.24 = (bf16[768]{0:T(1024)(128)(2,1)S(1)}, bf16[768]{0:T(1024)(128)(2,1)}, u32[]{:S(2)}) copy-start(bf16[768]{0:T(1024)(128)(2,1)} %get-tuple-element.28) | copy-start | bytes 4612
  142.2 3.3 %copy-start.36 = (bf16[768]{0:T(1024)(128)(2,1)S(1)}, bf16[768]{0:T(1024)(128)(2,1)}, u32[]{:S(2)}) copy-start(bf16[768]{0:T(1024)(128)(2,1)} %get-tuple-element.30) | copy-start | bytes 4612
  243.1 6.6 %copy-start.17 = (f32[16,256]{1,0:T(8,128)S(1)}, f32[16,256]{1,0:T(8,128)}, u32[]{:S(2)}) copy-start(f32[16,256]{1,0:T(8,128)} %get-tuple-element.27) | copy-start | bytes 49156

commit v2 on v1

--- a/solution.py
+++ b/solution.py
@@ -16,7 +16,7 @@
 NEGATIVE = -1e30
 MESH = pl.DeviceIdType.MESH
 SHAPES = ((D, 3 * D), (D, D), (D, FF), (FF, D))
-SMALL = 2 * D + 6 * D + FF
+LAG = 1
 HALVES = ((0, 1, 2), (0, 2, 1))
 
 
@@ -59,12 +59,27 @@
     pl.semaphore_wait(barrier, count)
 
 
-def half_cols(ref, half):
-    width = ref.shape[-1] // 2
-    return pl.ds(half * width, width)
-
-
-def gather_kernel(dims, n, *refs):
+def chunks_of(slabs, order):
+    chunks = []
+    for a in order:
+        rows, cols = slabs[a]
+        if rows >= 96 and rows % 32 == 0:
+            chunks += [(a, r, rows // 2, 0, cols) for r in (0, rows // 2)]
+        elif cols > 768 and cols % 768 == 0:
+            chunks += [(a, 0, rows, i * (cols // 3), cols // 3) for i in range(3)]
+        else:
+            chunks.append((a, 0, rows, 0, cols))
+    return chunks
+
+
+def window(chunk, half=None):
+    a, row, rows, col, cols = chunk
+    if half is None:
+        return pl.ds(row, rows), pl.ds(col, cols)
+    return pl.ds(row, rows), pl.ds(col + half * (cols // 2), cols // 2)
+
+
+def gather_kernel(dims, n, chunks, *refs):
     ins, outs = refs[:n], refs[n : 2 * n]
     local_sem, send_sem, recv_sem = refs[2 * n :]
     at, other = place(dims)
@@ -75,17 +90,20 @@
         copy.start()
         locals_.append(copy)
 
-    def send(a, half, phase):
-        cols = half_cols(outs[a], half)
+    waited = set()
+
+    def send(i, half, phase):
+        a = chunks[i][0]
+        view = window(chunks[i], half)
         order = HALVES[half]
         dim = order[phase]
         where = [slice(None) if d in order[:phase] else at[d] for d in range(4)]
         base = sum(dims[d] - 1 for d in order[:phase])
         copies = []
         for step in range(1, dims[dim]):
-            target = outs[a].at[tuple(where) + (slice(None), cols)]
-            source = ins[a].at[:, cols] if phase == 0 else target
-            sem = (a, half, base + step - 1)
+            target = outs[a].at[tuple(where) + view]
+            source = ins[a].at[view] if phase == 0 else target
+            sem = (i, half, base + step - 1)
             copy = pltpu.make_async_remote_copy(
                 source,
                 target,
@@ -101,36 +119,43 @@
     last = sum(dims[:3]) - 3
     flying, cores = {}, {}
 
-    def advance(a, phase):
-        if phase == 1:
+    def advance(i, phase):
+        a = chunks[i][0]
+        if phase == 1 and a not in waited:
+            waited.add(a)
             locals_[a].wait()
         if phase <= 2:
             for half in range(2):
                 if phase:
-                    for copy in flying[a, half, phase - 1]:
+                    for copy in flying[i, half, phase - 1]:
                         copy.wait_recv()
-                flying[a, half, phase] = send(a, half, phase)
+                flying[i, half, phase] = send(i, half, phase)
         elif phase == 3:
             for half in range(2):
-                for copy in flying[a, half, 2]:
+                for copy in flying[i, half, 2]:
                     copy.wait_recv()
-            block = outs[a].at[:, :, :, at[3]]
-            sem = (a, 0, last)
-            cores[a] = pltpu.make_async_remote_copy(
-                block, block, send_sem.at[sem], recv_sem.at[sem],
-                device_id=(other(3, 1)[1],), device_id_type=MESH,
+            block = outs[a].at[(slice(None),) * 3 + (at[3],) + window(chunks[i])]
+            sem = (i, 0, last)
+            cores[i] = pltpu.make_async_remote_copy(
+                block,
+                block,
+                send_sem.at[sem],
+                recv_sem.at[sem],
+                device_id=(other(3, 1)[1],),
+                device_id_type=MESH,
             )
-            cores[a].start()
+            cores[i].start()
         else:
-            cores[a].wait_recv()
-
-    for a in range(n):
-        advance(a, 0)
-    for t in range(n + 3):
+            cores[i].wait_recv()
+
+    count = len(chunks)
+    for i in range(count):
+        advance(i, 0)
+    for t in range(count + 3):
         for phase in range(1, 5):
-            a = t - phase + 1
-            if 0 <= a < n:
-                advance(a, phase)
+            i = t - phase + 1
+            if 0 <= i < count:
+                advance(i, phase)
     for copies in flying.values():
         for copy in copies:
             copy.wait_send()
@@ -138,18 +163,19 @@
         copy.wait_send()
 
 
-def gather(parts, dims):
+def gather(parts, dims, order):
     n = len(parts)
+    chunks = chunks_of([p.shape for p in parts], order)
     steps = sum(dims[:3]) - 2
     return pl.pallas_call(
-        functools.partial(gather_kernel, dims, n),
+        functools.partial(gather_kernel, dims, n, chunks),
         out_shape=[jax.ShapeDtypeStruct(dims + p.shape, p.dtype) for p in parts],
         in_specs=[pl.BlockSpec(memory_space=pl.ANY)] * n,
         out_specs=[pl.BlockSpec(memory_space=pl.ANY)] * n,
         scratch_shapes=[
             pltpu.SemaphoreType.DMA((n,)),
-            pltpu.SemaphoreType.DMA((n, 2, steps)),
-            pltpu.SemaphoreType.DMA((n, 2, steps)),
+            pltpu.SemaphoreType.DMA((len(chunks), 2, steps)),
+            pltpu.SemaphoreType.DMA((len(chunks), 2, steps)),
         ],
         compiler_params=pltpu.CompilerParams(collective_id=0, has_side_effects=True),
     )(*parts)
@@ -189,10 +215,37 @@
     return shapes
 
 
-def reduce_kernel(dims, n, *refs):
-    ins, outs = refs[:n], refs[n : 2 * n]
-    scratch = [refs[2 * n + 7 * a : 2 * n + 7 * a + 7] for a in range(n)]
-    send_sem, recv_sem = refs[9 * n :]
+def weight_gradient(left, right, turned, part):
+    rows, (slab_rows, cols) = left.shape[1], part.shape[4:]
+    step = 512 if rows <= D and cols % 512 == 0 else 256
+    flipped = turned.at[pl.ds(0, rows)]
+    flipped[...] = left[...].T
+    depth = min(rows, D)
+    lead = part.shape[0] * depth // rows
+
+    def body(j, carry):
+        view = pl.ds(pl.multiple_of(j * step, step), step)
+        for i in range(rows // depth):
+            value = jnp.dot(
+                turned[pl.ds(i * depth, depth)], right[:, view], preferred_element_type=jnp.float32
+            )
+            value = value.reshape((lead,) + part.shape[1:4] + (slab_rows, step))
+            part[pl.ds(i * lead, lead), :, :, :, :, view] = value.astype(part.dtype)
+        return carry
+
+    lax.fori_loop(0, cols // step, body, 0)
+
+
+def reduce_kernel(dims, n, chunks, fused, *refs):
+    count = len(chunks)
+    if fused:
+        pairs, given, refs = refs[: 2 * n - 2], refs[2 * n - 2], refs[2 * n - 1 :]
+        outs, parts, turned, refs = refs[:n], refs[n : 2 * n - 1], refs[2 * n - 1], refs[2 * n :]
+        ins = list(parts) + [given]
+    else:
+        ins, outs, refs = refs[:n], refs[n : 2 * n], refs[2 * n :]
+    scratch = [refs[7 * i : 7 * i + 7] for i in range(count)]
+    send_sem, recv_sem = refs[7 * count :]
     at, other = place(dims)
     greet(dims, other)
     last = sum(dims[:3]) - 3
@@ -207,7 +260,8 @@
 
     def held(a, half, phase):
         if phase == 0:
-            return scratch[a][0], [0, 1, 2], half_cols(scratch[a][0], half)
+            width = chunks[a][4] // 2
+            return scratch[a][0], [0, 1, 2], pl.ds(half * width, width)
         left = list(HALVES[half][: 3 - phase])
         return scratch[a][3 * half + phase].at[0], sorted(left), slice(None)
 
@@ -245,7 +299,7 @@
             (lambda where, s=s: landed.at[(s,) + tuple(where)]) for s in range(dims[dim] - 1)
         ]
         if phase == 3:
-            total = lambda where: outs[a].at[:, half_cols(outs[a], half)]
+            total = lambda where: outs[chunks[a][0]].at[window(chunks[a], half)]
         else:
             total = lambda where: landed.at[(0,) + tuple(where)]
         add_blocks(total, terms, [dims[d] for d in left])
@@ -253,7 +307,12 @@
     def advance(a, phase):
         if phase == 0:
             flying[a, 0, 0] = [
-                remote(ins[a].at[:, :, :, 1 - at[3]], scratch[a][0], (a, 0, last), other(3, 1)[1])
+                remote(
+                    ins[chunks[a][0]].at[(slice(None),) * 3 + (1 - at[3],) + window(chunks[a])],
+                    scratch[a][0],
+                    (a, 0, last),
+                    other(3, 1)[1],
+                )
             ]
             return
         if phase == 1:
@@ -261,7 +320,10 @@
                 copy.wait_recv()
             add_blocks(
                 lambda w: scratch[a][0].at[tuple(w)],
-                [lambda w: ins[a].at[tuple(w) + (at[3],)], lambda w: scratch[a][0].at[tuple(w)]],
+                [
+                    lambda w: ins[chunks[a][0]].at[tuple(w) + (at[3],) + window(chunks[a])],
+                    lambda w: scratch[a][0].at[tuple(w)],
+                ],
                 list(dims[:3]),
             )
         for half in range(2):
@@ -270,38 +332,49 @@
             if phase < 4:
                 push(a, half, phase)
 
-    for a in range(n):
-        advance(a, 0)
-    for t in range(n + 3):
+    made = set()
+    for t in range(count + LAG + 4):
+        if t < count:
+            array = chunks[t][0]
+            if fused and array not in made and array < n - 1:
+                weight_gradient(pairs[2 * array], pairs[2 * array + 1], turned, ins[array])
+            made.add(array)
+            advance(t, 0)
         for phase in range(1, 5):
-            a = t - phase + 1
-            if 0 <= a < n:
+            a = t - phase + 1 - LAG
+            if 0 <= a < count:
                 advance(a, phase)
     for copies in flying.values():
         for copy in copies:
             copy.wait_send()
 
 
-def reduce_scatter(parts, dims):
-    n = len(parts)
+def reduce_scatter(parts, pairs, dims, slabs, order):
+    n = len(slabs)
     steps = sum(dims[:3]) - 2
+    chunks = chunks_of(slabs, order)
     scratch = []
-    for p in parts:
-        scratch += [pltpu.VMEM(s, p.dtype) for s in reduce_scratch(dims, p.shape[4:])]
+    if pairs:
+        scratch += [pltpu.VMEM(dims + s, jnp.bfloat16) for s in slabs[:-1]]
+        scratch.append(pltpu.VMEM((FF, pairs[0].shape[0]), jnp.bfloat16))
+    for chunk in chunks:
+        shapes = reduce_scratch(dims, (chunk[2], chunk[4]))
+        scratch += [pltpu.VMEM(s, jnp.bfloat16) for s in shapes]
+    operands = list(pairs) + list(parts)
     return pl.pallas_call(
-        functools.partial(reduce_kernel, dims, n),
-        out_shape=[jax.ShapeDtypeStruct(p.shape[4:], jnp.float32) for p in parts],
-        in_specs=[pl.BlockSpec(memory_space=pltpu.VMEM)] * n,
+        functools.partial(reduce_kernel, dims, n, chunks, bool(pairs)),
+        out_shape=[jax.ShapeDtypeStruct(s, jnp.float32) for s in slabs],
+        in_specs=[pl.BlockSpec(memory_space=pltpu.VMEM)] * len(operands),
         out_specs=[pl.BlockSpec(memory_space=pltpu.VMEM)] * n,
         scratch_shapes=scratch
         + [
-            pltpu.SemaphoreType.DMA((n, 2, steps)),
-            pltpu.SemaphoreType.DMA((n, 2, steps)),
+            pltpu.SemaphoreType.DMA((len(chunks), 2, steps)),
+            pltpu.SemaphoreType.DMA((len(chunks), 2, steps)),
         ],
         compiler_params=pltpu.CompilerParams(
-            collective_id=1, has_side_effects=True, vmem_limit_bytes=60 * 2**20
+            collective_id=1, has_side_effects=True, vmem_limit_bytes=62 * 2**20
         ),
-    )(*parts)
+    )(*operands)
 
 
 def norm_forward(values, gain, shift):
@@ -379,14 +452,11 @@
     dy = live * cotangent.astype(jnp.float32)
     dyl = low(dy)
     du = low(dot(dyl, w_down, NT) * slope)
-    g_down = low(dot(z, dyl, TN))
     dh2 = dot(du, w_up, NT)
-    g_up = low(dot(h2, du, TN))
     back, gain2, shift2 = norm_backward(dh2, normal2, scale2, gains[1])
     dy1 = dy + back
     da = low(dy1)
     do = low(dot(da, w_out, NT)).reshape(rows, H, HD).transpose(1, 0, 2)
-    g_out = low(dot(o, da, TN))
     dp = bmm("hqe,hke->hqk", do, v)
     dv = low(bmm("hqk,hqe->hke", pb, do))
     ds = low(p * (dp - jnp.sum(p * dp, axis=-1, keepdims=True)))
@@ -395,7 +465,6 @@
     dmixed = jnp.concatenate(
         [a.transpose(1, 0, 2).reshape(rows, D) for a in (dq, dk, dv)], axis=1
     )
-    g_qkv = low(dot(h1, dmixed, TN))
     dh1 = dot(dmixed, w_qkv, NT)
     back, gain1, shift1 = norm_backward(dh1, normal1, scale1, gains[0])
     grad_tokens = low(dy1 + back)
@@ -403,7 +472,8 @@
     sums = jnp.concatenate(
         [shift1, shift2, f32(dmixed[:, :D]), f32(dmixed[:, 2 * D :]), f32(da), f32(dyl), f32(du)]
     )
-    return out, grad_tokens, (g_qkv, g_out, g_up, g_down), jnp.concatenate([gain1, gain2]), sums
+    pairs = (h1, dmixed, o, da, h2, du, z, dyl)
+    return out, grad_tokens, pairs, jnp.concatenate([gain1, gain2]), sums
 
 
 def shards(dims, tokens, lengths, cotangent, w_qkv, w_out, w_up, w_down, gains, biases):
@@ -413,24 +483,26 @@
     small = jnp.concatenate([gains, biases])
     small = jnp.pad(small, (0, 4096 - own_gain - own_bias))
     parts = [p.reshape(s) for p, s in zip((w_qkv, w_out, w_up, w_down, small), slabs)]
-    order = (4, 0, 1, 2, 3)
-    got = gather([parts[i] for i in order], dims)
-    got = [got[order.index(i)] for i in range(5)]
+    got = gather(parts, dims, (4, 1, 0, 2, 3))
     weights = [g.reshape(shape) for g, shape in zip(got[:4], SHAPES)]
     small = got[4].reshape(devices, 4096)
     gain_all = small[:, :own_gain].reshape(2, D).astype(jnp.float32)
     bias_all = small[:, own_gain : own_gain + own_bias].reshape(-1).astype(jnp.float32)
-    out, grad_tokens, grads, gain_sums, bias_sums = block(
+    out, grad_tokens, pairs, gain_sums, bias_sums = block(
         tokens, lengths, cotangent, weights, gain_all, bias_all[: 6 * D].reshape(6, D), bias_all[6 * D :]
     )
     small = jnp.concatenate(
         [gain_sums.reshape(devices, own_gain), bias_sums.reshape(devices, own_bias)], axis=1
     )
     small = low(jnp.pad(small, ((0, 0), (0, 4096 - own_gain - own_bias))))
-    parts = [g.reshape(dims + s) for g, s in zip(tuple(grads) + (small,), slabs)]
+    small = small.reshape(dims + slabs[4])
     order = (3, 2, 0, 1, 4)
-    sums = reduce_scatter([parts[i] for i in order], dims)
-    sums = [sums[order.index(i)] for i in range(5)]
+    if all(slab[1] == shape[1] for slab, shape in zip(slabs, SHAPES)):
+        sums = reduce_scatter([small], pairs, dims, slabs, order)
+    else:
+        grads = [low(dot(pairs[2 * i], pairs[2 * i + 1], TN)) for i in range(4)]
+        parts = [g.reshape(dims + s) for g, s in zip(grads, slabs)]
+        sums = reduce_scatter(parts + [small], (), dims, slabs, order)
     small = sums[4].reshape(-1)
     return (
         out,

time: 251 us -> 217 us (0.86)
  Pallas kernels: 182 us -> 164 us
  matrix products: 41.1 us -> 24.9 us
    pallas_call x2, Pallas kernels: 182 us -> 164 us  [the longest x1 86 us: gather(): pl.pallas_call(functools.partial(gather_kernel, dims, n, chunks), out_sha...]
    dot_general x12 -> x8, matrix products: 33 us -> 19.3 us  [dot(): lax.dot_general(a, b, (dims, ((), ())), preferred_element_type=jnp.float32)]
    unnamed x90 -> x64, local copies, waits for them, and re-layouts: 6.47 us -> 6.41 us
where the time goes in v2:
time: 217 us
  Pallas kernels  164 us (76%)
  matrix products  24.9 us (11%)
  local copies, waits for them, and re-layouts  22 us (10%)
  other arithmetic  4.13 us (2%)
    pallas_call x1, Pallas kernels, gather(): pl.pallas_call(functools.partial(gather_kernel, dims, n, chunks), out_sha...  86 us
    pallas_call x1, Pallas kernels, reduce_scatter(): pl.pallas_call(functools.partial(reduce_kernel, dims, n, chunks, bool(pai...  78.5 us
    dot_general x8, matrix products, dot(): lax.dot_general(a, b, (dims, ((), ())), preferred_element_type=jnp.float32)  19.3 us
    reshape x5, local copies, waits for them, and re-layouts, shards(): p.reshape(s)  7.13 us
    unnamed x64, local copies, waits for them, and re-layouts  6.41 us

profile of v2, /device:TPU:0, one launch (start us, length us, event | category | flops | bytes accessed | tf_op | source)
XLA Modules:
  0.0 216.7 jit_solution(12588151340102965027)
XLA Ops:
  0.6 1.7 reshape.266.refs_2_
  2.3 1.7 reshape.267.refs_3_
  4.0 1.7 reshape.264.refs_0_
  5.7 1.4 reshape.265.refs_1_
  7.2 0.7 fusion.44
  7.9 0.6 reshape.268.refs_4_
  8.5 86.0 %shard_map.152 = (bf16[4,2,2,2,24,2304]{5,4,3,2,1,0:T(8,128)(2,1)}, bf16[4,2,2,2,24,768]{5,4,3,2,1,0:T(8,128)(2,1)}, bf16[4,2,2,2,24,3072]{5,4,3,2,1,0:T(8,128)(...) custom-call(bf16[24,2304]{1,0:T(8,128)(2,1)} %reshape.264.refs_0_, ...), custom_call_target="tpu_custom_call" | custom-call | tf_op jit(solution)/shard_map/pallas_call | solution.py:170
  94.5 1.0 copy.45
  96.0 0.2 fusion.33
  96.4 2.7 %fusion.60 = f32[128,2304]{1,0:T(8,128)S(1)} fusion(bf16[128,768]{1,0:T(8,128)(2,1)S(1)} %fusion.26.refs_0_, bf16[768,2304]{1,0:T(8,128)(2,1)} %bitcast.79), kind=kOutput, calls=%fused_computation.115 | convolution fusion | flops 452984832 | bytes 4915200 | tf_op jit(solution)/shard_map/dot_general | solution.py:402
  99.6 0.2 copy-done.19
  99.8 0.2 slice_reduce_fusion
  100.4 1.3 fusion.57
  101.9 0.6 convolution_convert_fusion
  102.6 0.7 copy-done.1
  103.3 0.4 fusion.58
  103.7 0.2 multiply_reduce_fusion.3
  104.2 4.7 %multiply_convert_fusion = (bf16[128,3072]{1,0:T(8,128)(2,1)}, f32[128,3072]{1,0:T(8,128)S(1)}) fusion(f32[3072]{0:T(1024)S(1)} %slice.102, bf16[128,768]{1,0:T(8,128)(2,1)S(1)} %add_convert_fusion.refs_4_, bf16[768,3072]{1,0:T(8,128)(2,1)} %bitcast.69), kind=kOutput, calls=%fused_computation.11 | convolution fusion | flops 607911936 | bytes 7286784 | tf_op jit(solution)/shard_map/dot_general | solution.py:402
  109.1 1.8 fusion.59
  111.0 0.2 slice-done
  111.3 1.8 multiply_reduce_fusion.1
  113.2 0.2 fusion.54
  113.4 0.5 convolution_convert_fusion.2
  114.0 0.2 copy.33
  114.2 1.5 multiply_reduce_fusion
  115.9 0.3 bitcast_reduce_fusion.1
  116.3 0.4 fusion.14
  116.9 1.5 bitcast_reduce_fusion
  118.5 3.4 %fusion.32 = (bf16[768]{0:T(1024)(128)(2,1)S(1)}, f32[128]{0:T(128)S(1)}, f32[128]{0:T(128)S(1)}, bf16[768]{0:T(1024)(128)(2,1)S(1)}, f32[128,768]{1,0:T(8,128)S(1)}) fusion(bf16[128,768]{1,0:T(8,128)(2,1)S(1)} %copy-done, f32[128]{0:T(128)S(1)} %copy-done.21, f32[128]{0:T(128)S(1)} %copy-done.16, f32[768]{0:T(1024)S(1)} %mul.199, ...), kind=kOutput, calls=%fused_computation.51 | convolution fusion | flops 455735552 | bytes 4726784 | tf_op jit(solution)/shard_map/dot_general | solution.py:402
  121.9 0.4 dynamic-update-slice
  122.4 0.2 dynamic-update-slice.1
  122.7 0.2 dynamic-update-slice.2
  122.9 0.2 dynamic-update-slice.3
  123.1 0.2 dynamic-update-slice.4
  123.3 0.2 dynamic-update-slice.5
  123.5 0.2 dynamic-update-slice.6
  124.1 0.8 copy.46
  124.9 0.9 pad_maximum_fusion.refs_1_
  125.7 0.8 copy.40.refs_2_
  126.6 78.5 %shard_map.153 = (f32[24,2304]{1,0:T(8,128)}, f32[24,768]{1,0:T(8,128)}, f32[24,3072]{1,0:T(8,128)}, f32[96,768]{1,0:T(8,128)}, f32[16,256]{1,0:T(8,128)}) custom-call(bf16[128,768]{1,0:T(8,128)(2,1)} %copy-done.4, bf16[128,2304]{1,0:T(8,128)(2,1)} %pad_maximum_fusion.refs_1_, bf16[128,768]{1,0:T(8,128)(2,1)} %copy.40.refs_2_, bf16[128,768]{1,0:T(8,128)(2,1)} %copy-done.5, ...), custom_call_target="tpu_custom_call" | custom-call | tf_op jit(solution)/shard_map/pallas_call | solution.py:364
  205.1 1.8 copy.47
  206.9 1.7 reshape.287
  208.6 1.6 reshape.284
  210.2 0.6 reshape.285
  210.9 0.6 slice.105
  211.5 0.5 slice.104
  212.0 0.9 fusion.31
  212.9 3.8 %fusion.13 = bf16[128,768]{1,0:T(8,128)(2,1)} fusion(f32[128,768]{1,0:T(8,128)S(1)} %get-tuple-element.56, bf16[128,3072]{1,0:T(8,128)(2,1)S(1)} %copy-done.2, bf16[3072,768]{1,0:T(8,128)(2,1)} %bitcast.75, f32[768]{0:T(1024)S(1)} %get-tuple-element.45, f32[128]{0:T(128)S(1)} %copy-done.18), kind=kOutput, calls=%fused_computation.23 | convolution fusion | flops 604372992 | bytes 6098432 | tf_op jit(solution)/shard_map/dot_general | solution.py:402
  (96 shorter events, 3.3 us)
Async XLA Ops:
  0.6 95.2 %copy-start = (bf16[128,768]{1,0:T(8,128)(2,1)S(1)}, bf16[128,768]{1,0:T(8,128)(2,1)}, u32[]{:S(2)}) copy-start(bf16[128,768]{1,0:T(8,128)(2,1)} %param.9) | copy-start | bytes 589828
  96.0 3.1 %copy-start.15 = (f32[128]{0:T(128)}, f32[128]{0:T(128)S(1)}, u32[]{:S(2)}) copy-start(f32[128]{0:T(128)S(1)} %broadcast_multiply_fusion.5) | copy-start | bytes 1540
  96.2 2.9 %copy-start.20 = (f32[128]{0:T(128)}, f32[128]{0:T(128)S(1)}, u32[]{:S(2)}) copy-start(f32[128]{0:T(128)S(1)} %add_rsqrt_fusion.1) | copy-start | bytes 1540
  96.4 2.8 %copy-start.4 = (bf16[128,768]{1,0:T(8,128)(2,1)}, bf16[128,768]{1,0:T(8,128)(2,1)S(1)}, u32[]{:S(2)}) copy-start(bf16[128,768]{1,0:T(8,128)(2,1)S(1)} %fusion.26.refs_0_) | copy-start | bytes 589828
  99.1 0.7 copy-start.19
  100.4 2.1 copy-start.13
  101.9 0.7 copy-start.10
  101.9 1.3 copy-start.1
  104.0 5.1 %slice-start.2 = ((s8[4718592]{0:T(1024)(128)(4,1)}), s8[4194304]{0:T(1024)(128)(4,1)S(1)}, s32[]{:S(2)}) async-start(s8[4718592]{0:T(1024)(128)(4,1)} %bitcast.76), calls=%async_computation.2 | async-start | bytes 8388608
  104.2 4.8 %copy-start.9 = (bf16[128,768]{1,0:T(8,128)(2,1)}, bf16[128,768]{1,0:T(8,128)(2,1)S(1)}, u32[]{:S(2)}) copy-start(bf16[128,768]{1,0:T(8,128)(2,1)S(1)} %add_convert_fusion.refs_4_) | copy-start | bytes 589828
  104.2 4.7 %copy-start.7 = (bf16[128,768]{1,0:T(8,128)(2,1)S(1)}, bf16[128,768]{1,0:T(8,128)(2,1)}, u32[]{:S(2)}) copy-start(bf16[128,768]{1,0:T(8,128)(2,1)} %param.11) | copy-start | bytes 589828
  104.2 4.9 %slice-start.3 = ((s8[4718592]{0:T(1024)(128)(4,1)}), s8[524288]{0:T(1024)(128)(4,1)S(1)}, s32[]{:S(2)}) async-start(s8[4718592]{0:T(1024)(128)(4,1)} %bitcast.76), calls=%async_computation.3 | async-start | bytes 1048576
  108.9 4.2 %copy-start.17 = (f32[128]{0:T(128)}, f32[128]{0:T(128)S(1)}, u32[]{:S(2)}) copy-start(f32[128]{0:T(128)S(1)} %compare_convert_fusion.2) | copy-start | bytes 1540
  109.0 2.3 %slice-start = ((s8[4718592]{0:T(1024)(128)(4,1)}), s8[4194304]{0:T(1024)(128)(4,1)S(1)}, s32[]{:S(2)}) async-start(s8[4718592]{0:T(1024)(128)(4,1)} %bitcast.70), calls=%async_computation | async-start | bytes 8388608
  109.1 1.9 copy-start.8
  109.1 2.2 %slice-start.1 = ((s8[4718592]{0:T(1024)(128)(4,1)}), s8[524288]{0:T(1024)(128)(4,1)S(1)}, s32[]{:S(2)}) async-start(s8[4718592]{0:T(1024)(128)(4,1)} %bitcast.70), calls=%async_computation.1 | async-start | bytes 1048576
  111.0 2.2 copy-start.3
  113.2 1.0 copy-start.11
  113.4 2.3 %copy-start.5 = (bf16[128,768]{1,0:T(8,128)(2,1)}, bf16[128,768]{1,0:T(8,128)(2,1)S(1)}, u32[]{:S(2)}) copy-start(bf16[128,768]{1,0:T(8,128)(2,1)S(1)} %get-tuple-element.41.refs_3_) | copy-start | bytes 589828
  114.2 1.6 copy-start.6
  116.9 1.6 copy-start.16
  116.9 1.6 copy-start.21
  205.0 5.2 %copy-start.12 = (f32[24,768]{1,0:T(8,128)S(1)}, f32[24,768]{1,0:T(8,128)}, u32[]{:S(2)}) copy-start(f32[24,768]{1,0:T(8,128)} %get-tuple-element.24) | copy-start | bytes 221188
  205.0 5.8 %copy-start.14 = (f32[16,256]{1,0:T(8,128)S(1)}, f32[16,256]{1,0:T(8,128)}, u32[]{:S(2)}) copy-start(f32[16,256]{1,0:T(8,128)} %get-tuple-element.27) | copy-start | bytes 49156
  205.1 7.0 %copy-start.22 = (f32[128]{0:T(128)S(1)}, f32[128]{0:T(128)}, u32[]{:S(2)}) copy-start(f32[128]{0:T(128)} %copy-done.20) | copy-start | bytes 1540
  205.1 7.8 %copy-start.2 = (bf16[128,3072]{1,0:T(8,128)(2,1)S(1)}, bf16[128,3072]{1,0:T(8,128)(2,1)}, u32[]{:S(2)}) copy-start(bf16[128,3072]{1,0:T(8,128)(2,1)} %get-tuple-element.57.refs_6_) | copy-start | bytes 2359300
  205.1 7.8 %copy-start.18 = (f32[128]{0:T(128)S(1)}, f32[128]{0:T(128)}, u32[]{:S(2)}) copy-start(f32[128]{0:T(128)} %copy-done.17) | copy-start | bytes 1540
